TPU v7x, 32 devices: a whole 2x2x4 slice. The times are simulated.
32 devices in a mesh: ctx: 8 (over z, x), fsdp: 4 (over y, core).
Axes of the slice: x: 2, y: 2, z: 4, core: 2. Of those that a mesh axis runs over, the one named last changes fastest.
Arguments:
- tokens: bfloat16 [4, 2048, 8192], P('fsdp', 'ctx'), may hold values from -6 to 6
- queries: bfloat16 [4, 2048, 8192], P('fsdp', 'ctx'), may hold values from -384 to 384
- kv_weight: bfloat16 [8192, 2048], P(None, 'fsdp'), may hold values from -0.0625 to 0.0625
- block_list: int32 [8, 16, 8], replicated, may hold values from 0 to 15, as said below
- counts: int32 [8, 16], replicated, may hold values from 4 to 8, as said below
Outputs:
- attended: bfloat16 [4, 2048, 8192], P('fsdp', 'ctx')
Inputs may be any that keep to these rules, and one draw needn't show every extreme that they name: `block_list`: for each g and b the first counts[g, b] entries are distinct: block b, blocks b - 1 and b + 1 modulo 16 (the window wraps at the sequence's ends), the two global blocks of group g, and random blocks; the later entries are further distinct blocks. `counts`: some list has 8 live entries in every draw; loads differ from group to group.
All inputs are finite; a program needn't handle non-finite values.
Results may differ from a plain program's by a relative error of at most 0.007.
The roundings to bfloat16 on the way count: a program that leaves them out, or rounds other values in their place, can miss the bound.
Values may be sent and summed in bfloat16 or wider, within the bound.
No kernel may reach another device: no remote copies, remote signals or barrier semaphores. Data moves between devices by JAX's collectives and lax.ppermute only.
A program may use at most 192 MiB of HBM per device.

v0:
```python
import jax
import jax.numpy as jnp
from jax import lax
from jax.sharding import PartitionSpec as P

HQ = 64
KVH = 8
DH = 128
BLK = 128


def on_device(tokens, queries, kv_weight, block_list, counts):
    seq_rows = tokens.shape[1]
    n_ctx = lax.axis_size("ctx")
    kv_width = kv_weight.shape[1] * lax.axis_size("fsdp")
    pair_width = 2 * DH
    kv_heads = kv_width // pair_width
    copies = n_ctx // kv_heads
    column_part = jnp.einsum(
        "std,dc->stc",
        lax.all_gather(tokens, "fsdp", axis=0, tiled=True),
        kv_weight,
        preferred_element_type=jnp.float32,
    ).astype(jnp.bfloat16)
    keyvals = lax.all_to_all(column_part, "fsdp", split_axis=0, concat_axis=2, tiled=True)
    spread = jnp.broadcast_to(
        keyvals.reshape(1, seq_rows, kv_heads, 1, pair_width),
        (1, seq_rows, kv_heads, copies, pair_width),
    )
    spread = spread.reshape(1, seq_rows, kv_heads * copies * pair_width)
    query_local, keyval_local = (
        lax.all_to_all(queries, "ctx", split_axis=2, concat_axis=1, tiled=True),
        lax.all_to_all(spread, "ctx", split_axis=2, concat_axis=1, tiled=True),
    )
    head_count = query_local.shape[2] // DH
    length = query_local.shape[1]
    blocks = length // BLK
    kv_group = lax.axis_index("ctx") * head_count // (HQ // KVH)
    my_list = lax.dynamic_index_in_dim(block_list, kv_group, 0, keepdims=False)
    my_counts = lax.dynamic_index_in_dim(counts, kv_group, 0, keepdims=False)
    query_blocks = query_local.reshape(blocks, BLK, head_count, DH)
    keyval_blocks = keyval_local.reshape(blocks, BLK, pair_width)
    score_scale = DH ** (-0.5)
    slot_trips = jnp.max(my_counts)

    def slot_step(slot, state):
        row_top, row_total, weighted = state
        chosen = jnp.take(keyval_blocks, my_list[:, slot], axis=0)
        key_rows = chosen[:, :, :DH]
        value_rows = chosen[:, :, DH:]
        scores = (
            jnp.einsum("nqhd,nkd->nqhk", query_blocks, key_rows, preferred_element_type=jnp.float32)
            * score_scale
        )
        live_slot = (slot < my_counts)[:, None, None, None]
        scores = jnp.where(live_slot, scores, -jnp.inf)
        new_top = jnp.maximum(row_top, jnp.max(scores, axis=3))
        rescale = jnp.exp(row_top - new_top)
        weights = jnp.exp(scores - new_top[..., None])
        row_total = row_total * rescale + jnp.sum(weights, axis=3)
        update = jnp.einsum(
            "nqhk,nkd->nqhd",
            weights.astype(jnp.bfloat16),
            value_rows,
            preferred_element_type=jnp.float32,
        )
        weighted = weighted * rescale[..., None] + update
        return (new_top, row_total, weighted)

    start_state = (
        jnp.full((blocks, BLK, head_count), -jnp.inf, jnp.float32),
        jnp.zeros((blocks, BLK, head_count), jnp.float32),
        jnp.zeros((blocks, BLK, head_count, DH), jnp.float32),
    )
    row_top, row_total, weighted = lax.fori_loop(0, slot_trips, slot_step, start_state)
    result = (
        (weighted / row_total[..., None]).astype(jnp.bfloat16).reshape(1, length, head_count * DH)
    )
    return lax.all_to_all(result, "ctx", split_axis=1, concat_axis=2, tiled=True)


def solution(mesh):
    return jax.shard_map(
        on_device,
        mesh=mesh,
        in_specs=(P("fsdp", "ctx", None), P("fsdp", "ctx", None), P(None, "fsdp"), P(), P()),
        out_specs=P("fsdp", "ctx", None),
        check_vma=False,
    )
```

profile of v0, /device:TPU:0, one launch (start us, length us, event | category | flops | bytes accessed | tf_op | source)
XLA Modules:
  0.0 691.5 jit_solution(565378929133805145)
XLA Ops:
  7.3 110.3 %all-gather.2.cloned.1.call-done = bf16[4,256,8192]{2,1,0:T(8,128)(2,1)} async-done(((bf16[1,256,8192]{2,1,0:T(8,128)(2,1)}), bf16[4,256,8192]{2,1,0:T(8,128)(2,1)}) %all-gather.2.cloned.1.call-update) | async-done | bytes 16777232 | tf_op jit(solution)/shard_map/all_gather | solution.py:21
  117.6 15.5 %fusion.16 = bf16[4,256,512]{2,1,0:T(8,128)(2,1)} fusion(bf16[4,256,8192]{2,1,0:T(8,128)(2,1)} %all-gather.2.cloned.1.call-done, bf16[8192,512]{1,0:T(8,128)(2,1)} %param.9), kind=kOutput, calls=%fused_computation.28 | convolution fusion | flops 8590458880 | bytes 26214400 | tf_op jit(solution)/shard_map/std,dc->stc/dot_general | solution.py:19
  136.6 17.8 %copy.35 = bf16[1,256,8192]{1,0,2:T(2,128)(2,1)} copy(bf16[1,256,8192]{2,1,0:T(8,128)(2,1)} %param.8) | data formatting | bytes 8388608 | tf_op args[1]
  155.0 43.4 %reduce.2 = bf16[8192,256]{1,0:T(8,128)(2,1)} reduce(bf16[8192,1,256]{2,1,0:T(2,128)(2,1)} %bitcast.87, bf16[]{:T(256)} %broadcast.44), dimensions={1}, to_apply=%bitcast.58.reduce_sub_computation | reduce | bytes 8388610
  198.4 7.0 %reshape.38 = bf16[8,2,131072]{2,1,0:T(2,128)(2,1)} reshape(bf16[8192,256]{1,0:T(8,128)(2,1)} %reduce.2) | data formatting | bytes 8388608
  205.4 5.5 all-to-all-start.2
  211.4 11.7 %copy.50 = bf16[1,256,2048]{1,0,2:T(2,128)(2,1)S(1)} copy(bf16[1,256,2048]{1,2,0:T(8,128)(2,1)S(1)} %bitcast.98) | data formatting | bytes 2097152 | tf_op jit(solution)/shard_map/all_to_all | solution.py:25
  223.2 10.5 %reduce.1 = bf16[2048,256]{1,0:T(8,128)(2,1)S(1)} reduce(bf16[2048,1,256]{2,1,0:T(2,128)(2,1)S(1)} %bitcast.97, bf16[]{:T(256)} %broadcast.44), dimensions={1}, to_apply=%bitcast.67.reduce_sub_computation | reduce | bytes 2097154
  234.8 69.9 %all-to-all-done.2 = bf16[8,2,131072]{2,1,0:T(2,128)(2,1)} async-done(((bf16[8,2,131072]{2,1,0:T(2,128)(2,1)}), bf16[8,2,131072]{2,1,0:T(2,128)(2,1)}, u32[]{:S(2)}, u32[]{:S(2)}) %all-to-all-start.2) | async-done | bytes 4194336 | tf_op jit(solution)/shard_map/all_to_all | solution.py:32
  304.8 3.7 all-to-all-start.1
  309.9 8.8 %reshape.39 = bf16[8192,1,256]{2,1,0:T(2,128)(2,1)} reshape(bf16[8,2,131072]{2,1,0:T(2,128)(2,1)} %all-to-all-done.2) | data formatting | bytes 8388608
  318.7 6.1 copy.46
  324.8 6.5 copy.36
  339.6 4.3 broadcast_in_dim.37
  343.9 126.7 %while.14 = (s32[]{:T(128)}, f32[16,128,8]{1,2,0:T(8,128)S(1)}, f32[16,128,8]{1,2,0:T(8,128)S(1)}, f32[16,128,8,128]{3,1,2,0:T(8,128)}, s32[]{:T(128)}, /*index=...) while((s32[]{:T(128)}, f32[16,128,8]{1,2,0:T(8,128)S(1)}, ...), condition=%wide.region_4.5_spmd, body=%wide.region_1.4_spmd.sunk | while | flops 1101563008 | bytes 111154800 | solution.py:75
  351.9 6.8 multiply_add_fusion.5
  369.9 6.8 multiply_add_fusion.5
  387.8 6.8 multiply_add_fusion.5
  405.8 6.8 multiply_add_fusion.5
  423.8 6.8 multiply_add_fusion.5
  441.8 6.8 multiply_add_fusion.5
  459.7 6.8 multiply_add_fusion.5
  470.6 5.3 divide_convert_fusion
  475.9 5.6 copy.38
  481.5 23.8 %reshape.35 = bf16[1,2048,1024]{2,0,1:T(2,128)(2,1)} reshape(bf16[16,128,8,128]{3,2,1,0:T(8,128)(2,1)} %copy.38) | data formatting | bytes 8388608 | tf_op jit(solution)/shard_map/reshape | solution.py:77
  505.3 25.9 %reduce.3 = bf16[2048,1024]{1,0:T(8,128)(2,1)} reduce(bf16[2048,1,1024]{2,1,0:T(2,128)(2,1)} %bitcast.88, bf16[]{:T(256)} %broadcast.44), dimensions={1}, to_apply=%bitcast.60.reduce_sub_computation | reduce | bytes 8388610
  531.2 7.8 %reshape.40 = bf16[8,2,131072]{2,1,0:T(2,128)(2,1)} reshape(bf16[2048,1024]{1,0:T(8,128)(2,1)} %reduce.3) | data formatting | bytes 8388608
  539.0 117.0 %all_to_all.66 = bf16[8,2,131072]{2,1,0:T(2,128)(2,1)} all-to-all(bf16[8,2,131072]{2,1,0:T(2,128)(2,1)} %reshape.40), channel_id=1, replica_groups=mesh['ctx'=8,'fsdp'=4] {'ctx'}, dimensions={0} | all-to-all | bytes 8388608 | tf_op jit(solution)/shard_map/all_to_all | solution.py:79
  656.0 8.8 %reshape.41 = bf16[2048,1,1024]{2,1,0:T(2,128)(2,1)} reshape(bf16[8,2,131072]{2,1,0:T(2,128)(2,1)} %all_to_all.66) | data formatting | bytes 8388608
  664.8 7.1 %copy.47 = bf16[1,2048,1024]{2,1,0:T(8,128)(2,1)} copy(bf16[1,2048,1024]{2,0,1:T(2,128)(2,1)} %bitcast.90) | data formatting | bytes 8388608
  671.9 6.5 copy.40
  678.4 6.3 copy.41
  (140 shorter events, 88.8 us)
Async XLA Ops:
  6.5 303.4 %copy-start = (s32[8,16,8]{1,2,0:T(8,128)S(1)}, s32[8,16,8]{1,2,0:T(8,128)}, u32[]{:S(2)}) copy-start(s32[8,16,8]{1,2,0:T(8,128)} %param.10) | copy-start | bytes 12292
  6.5 111.0 %all-gather.2.cloned.1.call-start = ((), (), s32[]{:S(2)}) async-start(), calls=%async_computation.4 | async-start | bytes 20971520 | tf_op jit(solution)/shard_map/all_gather | solution.py:21
  133.1 72.2 %all-to-all-start = ((bf16[4,256,512]{2,1,0:T(8,128)(2,1)}), bf16[4,256,512]{2,1,0:T(8,128)(2,1)S(1)}, u32[]{:S(2)}, u32[]{:S(2)}) async-start(bf16[4,256,512]{2,1,0:T(8,128)(2,1)} %fusion.16), calls=%async_computation | async-start | bytes 2097152 | tf_op jit(solution)/shard_map/all_to_all | solution.py:25
  205.4 99.4 %all-to-all-start.2 = ((bf16[8,2,131072]{2,1,0:T(2,128)(2,1)}), bf16[8,2,131072]{2,1,0:T(2,128)(2,1)}, u32[]{:S(2)}, u32[]{:S(2)}) async-start(bf16[8,2,131072]{2,1,0:T(2,128)(2,1)} %reshape.38), calls=%async_computation.2 | async-start | bytes 8388608 | tf_op jit(solution)/shard_map/all_to_all | solution.py:32
  304.8 33.1 %all-to-all-start.1 = ((bf16[8,2,32768]{2,1,0:T(2,128)(2,1)}), bf16[8,2,32768]{2,1,0:T(2,128)(2,1)S(1)}, u32[]{:S(2)}, u32[]{:S(2)}) async-start(bf16[8,2,32768]{2,1,0:T(2,128)(2,1)} %reshape.36), calls=%async_computation.1 | async-start | bytes 2097152 | tf_op jit(solution)/shard_map/all_to_all | solution.py:33
  345.3 6.6 slice-start
  345.5 6.4 slice-start.1
  358.7 3.2 copy-start.2
  363.3 6.6 slice-start
  363.4 6.4 slice-start.1
  376.6 3.2 copy-start.2
  381.2 6.6 slice-start
  381.4 6.4 slice-start.1
  394.6 3.2 copy-start.2
  399.2 6.6 slice-start
  399.4 6.4 slice-start.1
  412.6 3.2 copy-start.2
  417.2 6.6 slice-start
  417.3 6.4 slice-start.1
  430.6 3.2 copy-start.2
  435.1 6.6 slice-start
  435.3 6.4 slice-start.1
  448.5 3.2 copy-start.2
  453.1 6.6 slice-start
  453.3 6.4 slice-start.1
  466.5 3.2 copy-start.2
  671.9 12.8 %copy-start.1 = (s32[8,16,8]{1,2,0:T(8,128)S(1)}, s32[8,16,8]{1,2,0:T(8,128)}, u32[]{:S(2)}) copy-start(s32[8,16,8]{1,2,0:T(8,128)} %param.10) | copy-start | bytes 12292
Sparse Core Ops, SparseCore 0:
  8.9 108.6 all-gather.1
where the time goes:
time: 694 us; the launch traced here: 692 us
  waiting for transfers between devices  181 us (26%)
  local copies, waits for them, and re-layouts  165 us (24%)
  blocking collectives  117 us (17%)
  other arithmetic  107 us (15%)
  matrix products  88.6 us (13%)
  between operations  13.5 us (2%)
  starting transfers between devices  12.8 us (2%)
    all_to_all x1, blocking collectives, on_device(): lax.all_to_all(result, 'ctx', split_axis=1, concat_axis=2, tiled=True)  117 us
    all_gather x1, waiting for transfers between devices, on_device(): lax.all_gather(tokens, 'fsdp', axis=0, tiled=True)  110 us
    unnamed x3, other arithmetic  79.9 us
    all_to_all x1, waiting for transfers between devices, on_device(): lax.all_to_all(queries, 'ctx', split_axis=2, concat_axis=1, tiled=True)  69.9 us
    unnamed x16, local copies, waits for them, and re-layouts  69.5 us
    dot_general x7, matrix products, slot_step(): jnp.einsum('nqhk,nkd->nqhd', weights.astype(jnp.bfloat16), value_rows, pr...  47.3 us
    dot_general x7, matrix products, slot_step(): jnp.einsum('nqhd,nkd->nqhk', query_blocks, key_rows, preferred_element_ty...  25.7 us
    reshape x1, local copies, waits for them, and re-layouts, on_device(): (weighted / row_total[..., None]).astype(jnp.bfloat16)  23.8 us
  transfers between devices with their start and end apart: 4, of which 2 were waited for; matrix products, arithmetic and copies ran while one was open for 18% of the time, Pallas kernels for 0%

commit v1 on v0

v1 whole, which is shorter than its diff:
```python
import functools

import jax
import jax.numpy as jnp
from jax import lax
from jax.experimental import pallas as pl
from jax.experimental.pallas import tpu as pltpu
from jax.sharding import PartitionSpec as P

DH = 128
BLK = 128
PAIR = 2 * DH
GROUP_HEADS = 8
GROUP_WIDTH = GROUP_HEADS * DH
LOG2E = 1.4426950408889634
SHARES = (8, 5, 3)

KERNEL_VMEM = 48 << 20
COST = pl.CostEstimate(flops=1, bytes_accessed=1, transcendentals=0)


def swap(array, axis, bit):
    size = lax.axis_size(axis)
    return lax.ppermute(array, axis, [(i, i ^ bit) for i in range(size)])


def rotate(array, steps, column_bit=0):
    n_ctx, n_col = lax.axis_size("ctx"), lax.axis_size("fsdp")
    order = []
    for c in range(n_ctx):
        to = (c + 2 * steps) % n_ctx
        order += [(c * n_col + f, to * n_col + (f ^ column_bit)) for f in range(n_col)]
    return lax.ppermute(array, ("ctx", "fsdp"), order)


def pin(mark, *arrays):
    return lax.optimization_barrier((mark, *arrays))


def turn_steps():
    pairs = lax.axis_size("ctx") // 2
    return sorted(range(1, pairs), key=lambda r: min(r, pairs - r))


def turn_all(array):
    return [rotate(array, r) for r in turn_steps()]


def cross(array):
    return swap(array, "ctx", 1)


def project_kernel(n_weights, tile, row_ref, *refs):
    weight_refs = refs[:n_weights]
    out_ref, held, total, sems = refs[-4:]
    width = weight_refs[0].shape[1]
    depth = row_ref.shape[1]
    copies = []
    for k in range(depth // tile):
        for i in range(n_weights):
            copies.append(
                pltpu.make_async_copy(
                    weight_refs[i].at[pl.ds(k * tile, tile)],
                    held.at[i, pl.ds(k * tile, tile)],
                    sems.at[k * n_weights + i],
                )
            )
    for copy in copies:
        copy.start()
    for k in range(depth // tile):
        for i in range(n_weights):
            copies[k * n_weights + i].wait()
            product = jnp.dot(
                row_ref[:, k * tile : (k + 1) * tile],
                held[i, k * tile : (k + 1) * tile, :],
                preferred_element_type=jnp.float32,
            )
            columns = slice(i * width, (i + 1) * width)
            if k == 0:
                total[:, columns] = product
            elif k + 1 < depth // tile:
                total[:, columns] += product
            else:
                out_ref[:, columns] = (total[:, columns] + product).astype(jnp.bfloat16)


def project(rows, weights):
    n_rows, depth = rows.shape
    width = weights[0].shape[1]
    tile = 1024
    n_weights = len(weights)
    out_width = width * n_weights
    inside = pl.BlockSpec(memory_space=pltpu.VMEM)
    return pl.pallas_call(
        functools.partial(project_kernel, n_weights, tile),
        out_shape=jax.ShapeDtypeStruct((n_rows, out_width), jnp.bfloat16),
        in_specs=[inside] + [pl.BlockSpec(memory_space=pltpu.HBM)] * n_weights,
        out_specs=inside,
        scratch_shapes=[
            pltpu.VMEM((n_weights, depth, width), jnp.bfloat16),
            pltpu.VMEM((n_rows, out_width), jnp.float32),
            pltpu.SemaphoreType.DMA((depth // tile * n_weights,)),
        ],
        cost_estimate=COST,
        compiler_params=pltpu.CompilerParams(vmem_limit_bytes=KERNEL_VMEM),
    )(rows, *weights)


def attend_blocks(live, q_ref, row_at, state_at, key_rows, value_rows, state_in, results):
    scale = DH ** (-0.5) * LOG2E
    keys = key_rows[: live * BLK, :]
    values = value_rows[: live * BLK, :].astype(jnp.float32).T.astype(jnp.bfloat16)
    for head in range(GROUP_HEADS):
        columns = slice(head * DH, (head + 1) * DH)
        q = q_ref[pl.ds(row_at, BLK), columns]
        scores = lax.dot_general(
            keys, q, (((1,), (1,)), ((), ())), preferred_element_type=jnp.float32
        )
        top = jnp.max(scores, axis=0, keepdims=True)
        weights = jnp.exp2((scores - top) * scale)
        total = jnp.sum(weights, axis=0, keepdims=True)
        mixed = jnp.dot(values, weights.astype(jnp.bfloat16), preferred_element_type=jnp.float32)
        if len(results) == 2:
            results[0][state_at * GROUP_HEADS + head] = mixed
            results[1][state_at * GROUP_HEADS + head, 0:1] = top
            results[1][state_at * GROUP_HEADS + head, 1:2] = total
            continue
        if state_in:
            other = state_in[1][state_at * GROUP_HEADS + head]
            other_top, other_total = other[0:1], other[1:2]
            both = jnp.maximum(top, other_top)
            here, there = jnp.exp2((top - both) * scale), jnp.exp2((other_top - both) * scale)
            total = total * here + other_total * there
            mixed = mixed * here + state_in[0][state_at * GROUP_HEADS + head] * there
        results[0][pl.ds(row_at, BLK), columns] = (mixed / total).T.astype(jnp.bfloat16)


def attend_kernel(places, shape, first_group, part, resumes, group_ref, list_ref, count_ref, me_ref, q_ref, *refs):
    held, q_held, key_rows, value_rows, sems = refs[-5:]
    blocks, max_live, local_blocks = shape
    state_in = refs[len(places) : len(places) + 2] if resumes else ()
    results = refs[-7:-5] if part == 0 else refs[-6:-5]
    held_rows = local_blocks * BLK if part is None else BLK
    pairs = held.shape[1] // (2 * held_rows)
    step, me = pl.program_id(0), me_ref[0]
    n_steps = pl.num_programs(0)

    def copies(index, slot):
        q_at = pl.multiple_of(group_ref[index] * GROUP_WIDTH, GROUP_WIDTH)
        made = [
            pltpu.make_async_copy(
                q_ref.at[:, pl.ds(q_at, GROUP_WIDTH)], q_held.at[slot], sems.at[slot, 0]
            )
        ]
        columns = pl.ds(pl.multiple_of((first_group + index) * PAIR, PAIR), PAIR)
        for ref, place in zip(refs, places):
            at = 0
            for back, member, row_at, rows in place:
                pair = lax.rem(me // 2 + pairs - back, pairs)
                start = pl.multiple_of((2 * pair + member) * held_rows + row_at, 16)
                made.append(
                    pltpu.make_async_copy(
                        ref.at[pl.ds(at, rows), columns],
                        held.at[slot, pl.ds(start, rows)],
                        sems.at[slot, len(made)],
                    )
                )
                at += rows
        return made

    slot = lax.rem(step, 2)

    @pl.when(step == 0)
    def _():
        for copy in copies(step, slot):
            copy.start()

    @pl.when(step + 1 < n_steps)
    def _():
        for copy in copies(step + 1, 1 - slot):
            copy.start()

    for copy in copies(step, slot):
        copy.wait()

    def one_block(block, carry):
        row_at = pl.multiple_of(block * BLK, BLK)
        entry = group_ref[step] * blocks + me * local_blocks + block
        count = count_ref[entry]
        taken = jnp.int32(0)
        for j in range(max_live):
            listed = list_ref[entry * max_live + j]
            source, inside = listed // local_blocks, lax.rem(listed, local_blocks)
            member = lax.rem(source + me, 2)
            from_row = (source // 2 * 2 + member) * held_rows
            wanted = j < count
            if part is None:
                from_row += inside * BLK
            else:
                wanted = jnp.logical_and(wanted, inside == part)
            from_row = pl.multiple_of(from_row, BLK)
            to_row = pl.multiple_of(taken * BLK, BLK)

            @pl.when(wanted)
            def _(from_row=from_row, to_row=to_row):
                chosen = held[slot, pl.ds(from_row, BLK), :]
                key_rows[pl.ds(to_row, BLK), :] = chosen[:, :DH]
                value_rows[pl.ds(to_row, BLK), :] = chosen[:, DH:]

            taken = taken + wanted.astype(jnp.int32)
        for live in range(4, max_live + 1) if part is None else range(1, max_live):
            pl.when(taken == live)(
                functools.partial(
                    attend_blocks,
                    live,
                    q_held.at[slot],
                    row_at,
                    block,
                    key_rows,
                    value_rows,
                    state_in,
                    results,
                )
            )
        return carry

    lax.fori_loop(0, local_blocks, one_block, 0)


def attend(queries, pieces, groups, first_group, block_list, counts, so_far, part=None, state=()):
    n_groups = groups.shape[0]
    rows, width = queries.shape
    local_blocks = rows // BLK
    blocks, max_live = block_list.shape[1:]
    places = [parts for _, parts in pieces]
    held_rows = sum(entry[-1] for parts in places for entry in parts)
    n_copies = 1 + sum(len(parts) for parts in places)
    me = lax.axis_index("ctx").astype(jnp.int32).reshape(1)
    anywhere = pl.BlockSpec(memory_space=pltpu.HBM)
    scalars = [groups, block_list.reshape(-1), counts.reshape(-1), me]
    operands = [queries] + [p for p, _ in pieces]
    in_specs = [anywhere] * len(operands)
    state_shapes = [
        (n_groups * local_blocks * GROUP_HEADS, DH, BLK),
        (n_groups * local_blocks * GROUP_HEADS, 8, BLK),
    ]
    state_specs = [
        pl.BlockSpec((local_blocks * GROUP_HEADS, *shape[1:]), lambda i, *_: (i, 0, 0))
        for shape in state_shapes
    ]
    operands += state
    in_specs += state_specs[: len(state)]
    aliases = {}
    if so_far is not None:
        aliases = {len(scalars) + len(operands): 0}
        operands.append(so_far)
        in_specs.append(anywhere)
    if part == 0:
        out_shape = [jax.ShapeDtypeStruct(shape, jnp.float32) for shape in state_shapes]
        out_specs = state_specs
    else:
        out_shape = jax.ShapeDtypeStruct((rows, width), jnp.bfloat16)
        out_specs = pl.BlockSpec((rows, GROUP_WIDTH), lambda i, g, *_: (0, g[i]))
    return pl.pallas_call(
        functools.partial(
            attend_kernel, places, (blocks, max_live, local_blocks), first_group, part, bool(state)
        ),
        out_shape=out_shape,
        grid_spec=pltpu.PrefetchScalarGridSpec(
            num_scalar_prefetch=len(scalars),
            grid=(n_groups,),
            in_specs=in_specs,
            out_specs=out_specs,
            scratch_shapes=[
                pltpu.VMEM((2, held_rows, PAIR), jnp.bfloat16),
                pltpu.VMEM((2, rows, GROUP_WIDTH), jnp.bfloat16),
                pltpu.VMEM((max_live * BLK, DH), jnp.bfloat16),
                pltpu.VMEM((max_live * BLK, DH), jnp.bfloat16),
                pltpu.SemaphoreType.DMA((2, n_copies)),
            ],
        ),
        input_output_aliases=aliases,
        cost_estimate=COST,
        compiler_params=pltpu.CompilerParams(vmem_limit_bytes=KERNEL_VMEM),
    )(*scalars, *operands)


def on_device(tokens, queries, kv_weight, block_list, counts):
    rows = tokens.shape[1]
    tokens = tokens.reshape(rows, -1)
    queries = queries.reshape(rows, -1)
    col = lax.axis_index("fsdp")
    local_groups = kv_weight.shape[1] // PAIR

    def groups_of(column):
        return column * local_groups + jnp.arange(local_groups, dtype=jnp.int32)

    def attend_to(groups, pieces, half, so_far, part=None, state=()):
        at = half * local_groups
        return attend(queries, pieces, groups, at, block_list, counts, so_far, part, state)

    def line(arrays, backs, place, member):
        return [(p, [(r, member, *place)]) for r, p in zip(backs, arrays)]

    at_second = SHARES[0] * rows // 16
    at_last = (SHARES[0] + SHARES[1]) * rows // 16
    n_turned = at_last - at_second
    steps = turn_steps()
    whole, early = (0, rows), (0, at_second)
    middle, late = (at_second, n_turned), (at_last, rows - at_last)
    pairs = lax.axis_size("ctx") // 2
    mark = jnp.zeros((8, 128), jnp.float32)

    first_got = swap(tokens[:at_second], "fsdp", 2)
    second_out = tokens[at_second:]
    weights = (kv_weight, swap(kv_weight, "fsdp", 1))
    side = project(tokens, weights)

    mark, side, second_out = pin(mark, side, second_out)
    side_turned = [rotate(side, r) for r in steps[:-1]]
    side_crossed = cross(side)
    second_got = swap(second_out, "fsdp", 2)
    mark, side, side_crossed = pin(mark, side, side_crossed)
    side_turned.append(rotate(side, steps[-1]))
    mark, first_got, *side_turned[:-1] = pin(mark, first_got, *side_turned[:-1])
    head_crossed = cross(jnp.concatenate(side_turned[:-1], axis=0))

    first = project(first_got, weights)
    mark, first = pin(mark, first)
    first = rotate(first, 1, 2)
    mark, first, side_turned[-1] = pin(mark, first, side_turned[-1])
    first_turned = turn_all(first)
    first_backs = [(1 + r) % pairs for r in [0, *steps]]
    mark, head_crossed = pin(mark, head_crossed)
    rest_crossed = cross(side_turned[-1])
    mark, rest_crossed, *first_turned = pin(mark, rest_crossed, *first_turned)
    first_crossed = cross(jnp.concatenate([first, *first_turned], axis=0))

    side_pieces = line([side, *side_turned], [0, *steps], whole, 0) + [
        (side_crossed, [(0, 1, *whole)]),
        (head_crossed, [(r, 1, *whole) for r in steps[:-1]]),
        (rest_crossed, [(steps[-1], 1, *whole)]),
    ]
    out = attend_to(groups_of(col), side_pieces, 0, None)
    mark, out, second_got = pin(mark, out, second_got)
    second = project(second_got, weights)
    mark, second = pin(mark, second)
    second = swap(second, "fsdp", 2)
    out = attend_to(groups_of(col ^ 1), side_pieces, 1, out)
    mark, out, second = pin(mark, out, second)

    turned = turn_all(second[:n_turned])
    last_pair = jnp.concatenate([second[n_turned:], cross(second[n_turned:])], axis=0)
    mark, last_pair, *turned = pin(mark, last_pair, *turned)
    crossed = cross(jnp.concatenate([second[:n_turned], *turned], axis=0))
    pair_turned = turn_all(last_pair)

    far_pieces = line([first, *first_turned], first_backs, early, 0)
    far_pieces.append((first_crossed, [(r, 1, *early) for r in first_backs]))
    far_pieces += line([second[:n_turned], *turned], [0, *steps], middle, 0)
    far_pieces.append((crossed, [(r, 1, *middle) for r in [0, *steps]]))
    for r, piece in zip([0, *steps], [last_pair, *pair_turned]):
        far_pieces.append((piece, [(r, 0, *late), (r, 1, *late)]))
    far_groups = jnp.concatenate([groups_of(col ^ 2), groups_of(col ^ 3)])
    out = attend_to(far_groups, far_pieces, 0, out)
    return out.reshape(1, rows, -1)


def solution(mesh):
    return jax.shard_map(
        on_device,
        mesh=mesh,
        in_specs=(P("fsdp", "ctx", None), P("fsdp", "ctx", None), P(None, "fsdp"), P(), P()),
        out_specs=P("fsdp", "ctx", None),
        check_vma=False,
    )
```

time: 694 us -> 202 us (0.29)
  local copies, waits for them, and re-layouts: 165 us -> 9.54 us
  blocking collectives: 117 us -> 0 us
  other arithmetic: 107 us -> 2.35 us
  waiting for transfers between devices: 181 us -> 85.2 us
  matrix products: 88.6 us -> 0 us
  Pallas kernels: 0 us -> 62.4 us
  starting transfers between devices: 12.8 us -> 40.6 us
  between operations: 13.5 us -> 0.34 us
    all_to_all x1 -> x0, blocking collectives: 117 us -> none  [on_device(): lax.all_to_all(result, 'ctx', split_axis=1, concat_axis=2, tiled=True)]
    all_gather x1 -> x0, waiting for transfers between devices: 110 us -> none  [on_device(): lax.all_gather(tokens, 'fsdp', axis=0, tiled=True)]
    dot_general x15 -> x0, matrix products: 88.6 us -> none  [the longest x7 47.3 us: slot_step(): jnp.einsum('nqhk,nkd->nqhd', weights.astype(jnp.bfloat16), value_rows, pr...]
    ppermute x0 -> x23, waiting for transfers between devices: none -> 85.2 us  [the longest x13 54.3 us: rotate(): return lax.ppermute(array, ('ctx', 'fsdp'), order)]
    unnamed x3 -> x0, other arithmetic: 79.9 us -> none
    all_to_all x3 -> x0, waiting for transfers between devices: 70 us -> none  [the longest x1 69.9 us: on_device(): lax.all_to_all(queries, 'ctx', split_axis=2, concat_axis=1, tiled=True)]
    unnamed x16 -> x9, local copies, waits for them, and re-layouts: 69.5 us -> 3.37 us
    pallas_call x0 -> x6, Pallas kernels: none -> 62.4 us  [the longest x3 40.9 us: attend(): pl.pallas_call(functools.partial(attend_kernel, places, (blocks, max_live...]
  transfers between devices with their start and end apart: 4 -> 23, of which waited for: 2 -> 11; matrix products, arithmetic and copies ran while one was open for 18% -> 4% of each run, Pallas kernels for 0% -> 17%
where the time goes in v1:
time: 202 us; the launch traced here: 200 us
  waiting for transfers between devices  85.2 us (42%)
  Pallas kernels  62.4 us (31%)
  starting transfers between devices  40.6 us (20%)
  local copies, waits for them, and re-layouts  9.54 us (5%)
  other arithmetic  2.35 us (1%)
    ppermute x13, waiting for transfers between devices, rotate(): return lax.ppermute(array, ('ctx', 'fsdp'), order)  54.3 us
    pallas_call x3, Pallas kernels, attend(): pl.pallas_call(functools.partial(attend_kernel, places, (blocks, max_live...  40.9 us
    ppermute x10, waiting for transfers between devices, swap(): return lax.ppermute(array, axis, [(i, i ^ bit) for i in range(size)])  30.9 us
    ppermute x13, starting transfers between devices, rotate(): return lax.ppermute(array, ('ctx', 'fsdp'), order)  26.7 us
    pallas_call x3, Pallas kernels, project(): pl.pallas_call(functools.partial(project_kernel, n_weights, tile), out_sh...  21.6 us
    ppermute x10, starting transfers between devices, swap(): return lax.ppermute(array, axis, [(i, i ^ bit) for i in range(size)])  13.9 us
    slice x1, local copies, waits for them, and re-layouts, on_device(): second_out = tokens[at_second:]  4.16 us
  transfers between devices with their start and end apart: 23, of which 11 were waited for; matrix products, arithmetic and copies ran while one was open for 4% of the time, Pallas kernels for 17%

profile of v1, /device:TPU:0, one launch (start us, length us, event | category | flops | bytes accessed | tf_op | source)
XLA Modules:
  0.0 200.4 jit_solution(10276117344313161293)
XLA Ops:
  0.5 4.2 %slice_bitcast_fusion = (bf16[128,8192]{1,0:T(8,128)(2,1)}, bf16[128,8192]{1,0:T(8,128)(2,1)S(1)}) fusion(bf16[1,256,8192]{2,1,0:T(8,128)(2,1)} %param.5), kind=kLoop, calls=%fused_computation | loop fusion | bytes 8388608 | tf_op jit(solution)/shard_map/slice | solution.py:315
  4.6 2.5 %collective-permute-start = (bf16[128,8192]{1,0:T(8,128)(2,1)S(1)}, bf16[128,8192]{1,0:T(8,128)(2,1)S(1)}, u32[]{:S(2)}, u32[]{:S(2)}) collective-permute-start(bf16[128,8192]{1,0:T(8,128)(2,1)S(1)} %get-tuple-element.48), channel_id=1, source_target_pairs={{0,2},{1,3},{2,0},{3,1},{4,6},{5,7},{6,4},{7,5},{8,10},{9,11},{10,... | collective-permute-start | bytes 6291464 | tf_op jit(solution)/shard_map/ppermute | solution.py:24
  7.1 6.3 %collective-permute-done.1.refs_1_ = bf16[8192,512]{1,0:T(8,128)(2,1)S(1)} collective-permute-done((bf16[8192,512]{1,0:T(8,128)(2,1)}, bf16[8192,512]{1,0:T(8,128)(2,1)S(1)}, u32[]{:S(2)}, u32[]{:S(2)}) %collective-permute-start.1) | collective-permute-done | bytes 8388640 | tf_op jit(solution)/shard_map/ppermute | solution.py:24
  13.5 3.3 %copy-done.1 = bf16[8192,512]{1,0:T(8,128)(2,1)} copy-done((bf16[8192,512]{1,0:T(8,128)(2,1)}, bf16[8192,512]{1,0:T(8,128)(2,1)S(1)}, u32[]{:S(2)}) %copy-start.1) | copy-done | bytes 8388632
  16.7 6.7 %shard_map.55.refs_0_ = bf16[256,1024]{1,0:T(8,128)(2,1)S(1)} custom-call(bf16[256,8192]{1,0:T(8,128)(2,1)S(1)} %bitcast.8, bf16[8192,512]{1,0:T(8,128)(2,1)} %refs_0_.5, bf16[8192,512]{1,0:T(8,128)(2,1)} %copy-done.1), custom_call_target="tpu_custom_call" | custom-call | flops 1 | bytes 1 | tf_op jit(solution)/shard_map/pallas_call | solution.py:94
  23.5 3.0 %collective-permute-start.13 = (bf16[128,8192]{1,0:T(8,128)(2,1)}, bf16[128,8192]{1,0:T(8,128)(2,1)}, u32[]{:S(2)}, u32[]{:S(2)}) collective-permute-start(bf16[128,8192]{1,0:T(8,128)(2,1)} %get-tuple-element.38), channel_id=1, source_target_pairs={{0,2},{1,3},{2,0},{3,1},{4,6},{5,7},{6,4},{7,5},{8,10},{9,11},{10,... | collective-permute-start | bytes 6291464 | tf_op jit(solution)/shard_map/ppermute | solution.py:24
  26.4 3.6 %collective-permute-start.3 = (bf16[256,1024]{1,0:T(8,128)(2,1)S(1)}, bf16[256,1024]{1,0:T(8,128)(2,1)S(1)}, u32[]{:S(2)}, u32[]{:S(2)}) collective-permute-start(bf16[256,1024]{1,0:T(8,128)(2,1)S(1)} %shard_map.55.refs_0_), channel_id=1, source_target_pairs={{0,24},{1,25},{2,26},{3,27},{4,28},{5,29},{6,30},{7,31},{8,0},{9,1... | collective-permute-start | bytes 1572872 | tf_op jit(solution)/shard_map/ppermute | solution.py:33
  30.1 1.5 collective-permute-start.5
  31.5 22.1 %collective-permute-done.row_ref = bf16[128,8192]{1,0:T(8,128)(2,1)S(1)} collective-permute-done((bf16[128,8192]{1,0:T(8,128)(2,1)S(1)}, bf16[128,8192]{1,0:T(8,128)(2,1)S(1)}, u32[]{:S(2)}, u32[]{:S(2)}) %collective-permute-start) | collective-permute-done | bytes 2097184 | tf_op jit(solution)/shard_map/ppermute | solution.py:24
  53.7 2.0 collective-permute-start.12
  55.7 2.6 %collective-permute-start.6 = (bf16[256,1024]{1,0:T(8,128)(2,1)S(1)}, bf16[256,1024]{1,0:T(8,128)(2,1)}, u32[]{:S(2)}, u32[]{:S(2)}) collective-permute-start(bf16[256,1024]{1,0:T(8,128)(2,1)S(1)} %shard_map.55.refs_0_), channel_id=1, source_target_pairs={{0,16},{1,17},{2,18},{3,19},{4,20},{5,21},{6,22},{7,23},{8,24},{9,... | collective-permute-start | bytes 1572872 | tf_op jit(solution)/shard_map/ppermute | solution.py:33
  58.3 6.3 %shard_map.56 = bf16[128,1024]{1,0:T(8,128)(2,1)S(1)} custom-call(bf16[128,8192]{1,0:T(8,128)(2,1)S(1)} %collective-permute-done.row_ref, bf16[8192,512]{1,0:T(8,128)(2,1)} %refs_0_.5, bf16[8192,512]{1,0:T(8,128)(2,1)} %copy-done.1), custom_call_target="tpu_custom_call" | custom-call | flops 1 | bytes 1 | tf_op jit(solution)/shard_map/pallas_call | solution.py:94
  64.6 2.6 %collective-permute-start.4 = (bf16[128,1024]{1,0:T(8,128)(2,1)S(1)}, bf16[128,1024]{1,0:T(8,128)(2,1)S(1)}, u32[]{:S(2)}, u32[]{:S(2)}) collective-permute-start(bf16[128,1024]{1,0:T(8,128)(2,1)S(1)} %shard_map.56), channel_id=1, source_target_pairs={{0,10},{1,11},{2,8},{3,9},{4,14},{5,15},{6,12},{7,13},{8,18},{9,19... | collective-permute-start | bytes 786440 | tf_op jit(solution)/shard_map/ppermute | solution.py:33
  67.2 10.1 %collective-permute-done.4.refs_0_ = bf16[128,1024]{1,0:T(8,128)(2,1)S(1)} collective-permute-done((bf16[128,1024]{1,0:T(8,128)(2,1)S(1)}, bf16[128,1024]{1,0:T(8,128)(2,1)S(1)}, u32[]{:S(2)}, u32[]{:S(2)}) %collective-permute-start.4) | collective-permute-done | bytes 262176 | tf_op jit(solution)/shard_map/ppermute | solution.py:33
  77.3 9.2 %collective-permute-done.6.refs_3_ = bf16[256,1024]{1,0:T(8,128)(2,1)} collective-permute-done((bf16[256,1024]{1,0:T(8,128)(2,1)S(1)}, bf16[256,1024]{1,0:T(8,128)(2,1)}, u32[]{:S(2)}, u32[]{:S(2)}) %collective-permute-start.6) | collective-permute-done | bytes 524320 | tf_op jit(solution)/shard_map/ppermute | solution.py:33
  87.0 3.5 %collective-permute-start.10 = (bf16[128,1024]{1,0:T(8,128)(2,1)S(1)}, bf16[128,1024]{1,0:T(8,128)(2,1)}, u32[]{:S(2)}, u32[]{:S(2)}) collective-permute-start(bf16[128,1024]{1,0:T(8,128)(2,1)S(1)} %collective-permute-done.4.refs_0_), channel_id=1, source_target_pairs={{0,16},{1,17},{2,18},{3,19},{4,20},{5,21},{6,22},{7,23},{8,24},{9,... | collective-permute-start | bytes 786440 | tf_op jit(solution)/shard_map/ppermute | solution.py:33
  90.5 2.0 %collective-permute-start.8 = (bf16[128,1024]{1,0:T(8,128)(2,1)S(1)}, bf16[128,1024]{1,0:T(8,128)(2,1)}, u32[]{:S(2)}, u32[]{:S(2)}) collective-permute-start(bf16[128,1024]{1,0:T(8,128)(2,1)S(1)} %collective-permute-done.4.refs_0_), channel_id=1, source_target_pairs={{0,8},{1,9},{2,10},{3,11},{4,12},{5,13},{6,14},{7,15},{8,16},{9,17... | collective-permute-start | bytes 786440 | tf_op jit(solution)/shard_map/ppermute | solution.py:33
  92.8 10.2 %collective-permute-done.10.refs_3_ = bf16[128,1024]{1,0:T(8,128)(2,1)} collective-permute-done((bf16[128,1024]{1,0:T(8,128)(2,1)S(1)}, bf16[128,1024]{1,0:T(8,128)(2,1)}, u32[]{:S(2)}, u32[]{:S(2)}) %collective-permute-start.10) | collective-permute-done | bytes 262176 | tf_op jit(solution)/shard_map/ppermute | solution.py:33
  103.1 6.3 %collective-permute-done.9.refs_2_ = bf16[128,1024]{1,0:T(8,128)(2,1)} collective-permute-done((bf16[128,1024]{1,0:T(8,128)(2,1)S(1)}, bf16[128,1024]{1,0:T(8,128)(2,1)}, u32[]{:S(2)}, u32[]{:S(2)}) %collective-permute-start.9) | collective-permute-done | bytes 262176 | tf_op jit(solution)/shard_map/ppermute | solution.py:33
  109.4 11.0 %shard_map.57.refs_7_ = bf16[256,8192]{1,0:T(8,128)(2,1)} custom-call(s32[2]{0:T(128)S(1)} %iota_add_fusion.group_ref, s32[1024]{0:T(1024)S(1)} %reshape.26.list_ref, s32[128]{0:T(128)S(1)} %reshape.27.count_ref, s32[1]{0:T(128)} %bitcast.me_ref, bf16[256,8192]{1,0:T(8,128)(2,1)} %bitcast.9, bf16[256,1024]{1,0:T(8,128)(2,1)S(1)} %shard_map.55.refs_0_, ...), custom_call_target="tpu_custom_call" | custom-call | flops 1 | bytes 1 | tf_op jit(solution)/shard_map/pallas_call | solution.py:264
  120.4 8.6 %shard_map.59 = bf16[128,1024]{1,0:T(8,128)(2,1)} custom-call(bf16[128,8192]{1,0:T(8,128)(2,1)} %collective-permute-done.13.row_ref, bf16[8192,512]{1,0:T(8,128)(2,1)} %refs_0_.5, bf16[8192,512]{1,0:T(8,128)(2,1)} %copy-done.1), custom_call_target="tpu_custom_call" | custom-call | flops 1 | bytes 1 | tf_op jit(solution)/shard_map/pallas_call | solution.py:94
  130.0 2.1 %pad_maximum_fusion = bf16[512,1024]{1,0:T(8,128)(2,1)} fusion(bf16[128,1024]{1,0:T(8,128)(2,1)} %collective-permute-done.10.refs_3_, bf16[128,1024]{1,0:T(8,128)(2,1)} %collective-permute-done.9.refs_2_, bf16[128,1024]{1,0:T(8,128)(2,1)} %collective-permute-done.8.refs_1_, bf16[128,1024]{1,0:T(8,128)(2,1)S(1)} %collective-permute-done.4.refs_0_), kind=kLoop, calls=%fused_computation.2 | loop fusion | flops 4194304 | bytes 2097152 | tf_op jit(solution)/shard_map/concatenate | solution.py:337
  132.9 10.2 %shard_map.58.refs_14_ = bf16[256,8192]{1,0:T(8,128)(2,1)} custom-call(s32[2]{0:T(128)S(1)} %iota_add_fusion.1.group_ref, s32[1024]{0:T(1024)S(1)} %reshape.26.list_ref, s32[128]{0:T(128)S(1)} %reshape.27.count_ref, s32[1]{0:T(128)} %bitcast.me_ref, bf16[256,8192]{1,0:T(8,128)(2,1)} %bitcast.10, ...), custom_call_target="tpu_custom_call", output_to_operand_aliasing={{}: (12, {})} | custom-call | flops 1 | bytes 1 | tf_op jit(solution)/shard_map/pallas_call | solution.py:264
  145.8 5.4 %collective-permute-start.18 = (bf16[80,1024]{1,0:T(8,128)(2,1)S(1)}, bf16[80,1024]{1,0:T(8,128)(2,1)S(1)}, u32[]{:S(2)}, u32[]{:S(2)}) collective-permute-start(bf16[80,1024]{1,0:T(8,128)(2,1)S(1)} %slice.25.refs_5_), channel_id=1, source_target_pairs={{0,16},{1,17},{2,18},{3,19},{4,20},{5,21},{6,22},{7,23},{8,24},{9,... | collective-permute-start | bytes 491528 | tf_op jit(solution)/shard_map/ppermute | solution.py:33
  151.3 2.3 %collective-permute-start.17 = (bf16[80,1024]{1,0:T(8,128)(2,1)S(1)}, bf16[80,1024]{1,0:T(8,128)(2,1)S(1)}, u32[]{:S(2)}, u32[]{:S(2)}) collective-permute-start(bf16[80,1024]{1,0:T(8,128)(2,1)S(1)} %slice.25.refs_5_), channel_id=1, source_target_pairs={{0,24},{1,25},{2,26},{3,27},{4,28},{5,29},{6,30},{7,31},{8,0},{9,1... | collective-permute-start | bytes 491528 | tf_op jit(solution)/shard_map/ppermute | solution.py:33
  153.6 2.5 %collective-permute-done.15 = bf16[48,1024]{1,0:T(8,128)(2,1)S(1)} collective-permute-done((bf16[48,1024]{1,0:T(8,128)(2,1)S(1)}, bf16[48,1024]{1,0:T(8,128)(2,1)S(1)}, u32[]{:S(2)}, u32[]{:S(2)}) %collective-permute-start.15) | collective-permute-done | bytes 98336 | tf_op jit(solution)/shard_map/ppermute | solution.py:24
  156.1 4.3 %collective-permute-done.18.refs_8_ = bf16[80,1024]{1,0:T(8,128)(2,1)S(1)} collective-permute-done((bf16[80,1024]{1,0:T(8,128)(2,1)S(1)}, bf16[80,1024]{1,0:T(8,128)(2,1)S(1)}, u32[]{:S(2)}, u32[]{:S(2)}) %collective-permute-start.18) | collective-permute-done | bytes 163872 | tf_op jit(solution)/shard_map/ppermute | solution.py:33
  160.4 2.8 %collective-permute-done.16.refs_6_ = bf16[80,1024]{1,0:T(8,128)(2,1)S(1)} collective-permute-done((bf16[80,1024]{1,0:T(8,128)(2,1)S(1)}, bf16[80,1024]{1,0:T(8,128)(2,1)S(1)}, u32[]{:S(2)}, u32[]{:S(2)}) %collective-permute-start.16) | collective-permute-done | bytes 163872 | tf_op jit(solution)/shard_map/ppermute | solution.py:33
  164.6 2.5 %collective-permute-start.22 = (bf16[96,1024]{1,0:T(8,128)(2,1)S(1)}, bf16[96,1024]{1,0:T(8,128)(2,1)S(1)}, u32[]{:S(2)}, u32[]{:S(2)}) collective-permute-start(bf16[96,1024]{1,0:T(8,128)(2,1)S(1)} %pad_maximum_fusion.3.refs_10_), channel_id=1, source_target_pairs={{0,16},{1,17},{2,18},{3,19},{4,20},{5,21},{6,22},{7,23},{8,24},{9,... | collective-permute-start | bytes 589832 | tf_op jit(solution)/shard_map/ppermute | solution.py:33
  169.3 8.3 %collective-permute-done.22.refs_13_ = bf16[96,1024]{1,0:T(8,128)(2,1)S(1)} collective-permute-done((bf16[96,1024]{1,0:T(8,128)(2,1)S(1)}, bf16[96,1024]{1,0:T(8,128)(2,1)S(1)}, u32[]{:S(2)}, u32[]{:S(2)}) %collective-permute-start.22) | collective-permute-done | bytes 196640 | tf_op jit(solution)/shard_map/ppermute | solution.py:33
  177.5 3.0 %collective-permute-done.21.refs_12_ = bf16[96,1024]{1,0:T(8,128)(2,1)S(1)} collective-permute-done((bf16[96,1024]{1,0:T(8,128)(2,1)S(1)}, bf16[96,1024]{1,0:T(8,128)(2,1)S(1)}, u32[]{:S(2)}, u32[]{:S(2)}) %collective-permute-start.21) | collective-permute-done | bytes 196640 | tf_op jit(solution)/shard_map/ppermute | solution.py:33
  180.6 19.6 %shard_map.60 = bf16[256,8192]{1,0:T(8,128)(2,1)} custom-call(s32[4]{0:T(128)S(1)} %pad_add_fusion.group_ref, s32[1024]{0:T(1024)S(1)} %reshape.26.list_ref, s32[128]{0:T(128)S(1)} %reshape.27.count_ref, s32[1]{0:T(128)} %bitcast.me_ref, bf16[256,8192]{1,0:T(8,128)(2,1)} %bitcast.11, ...), custom_call_target="tpu_custom_call", output_to_operand_aliasing={{}: (19, {})} | custom-call | flops 1 | bytes 1 | tf_op jit(solution)/shard_map/pallas_call | solution.py:264
  (42 shorter events, 9.4 us)
Async XLA Ops:
  0.0 13.4 %collective-permute-start.1 = (bf16[8192,512]{1,0:T(8,128)(2,1)}, bf16[8192,512]{1,0:T(8,128)(2,1)S(1)}, u32[]{:S(2)}, u32[]{:S(2)}) collective-permute-start(bf16[8192,512]{1,0:T(8,128)(2,1)} %refs_0_.5), channel_id=1, source_target_pairs={{0,1},{1,0},{2,3},{3,2},{4,5},{5,4},{6,7},{7,6},{8,9},{9,8},{10,11... | collective-permute-start | bytes 25165832 | tf_op jit(solution)/shard_map/ppermute | solution.py:24
  0.5 16.3 %copy-start = (bf16[1,256,8192]{2,1,0:T(8,128)(2,1)S(1)}, bf16[1,256,8192]{2,1,0:T(8,128)(2,1)}, u32[]{:S(2)}) copy-start(bf16[1,256,8192]{2,1,0:T(8,128)(2,1)} %param.5) | copy-start | bytes 12582916
  4.6 49.0 %collective-permute-start = (bf16[128,8192]{1,0:T(8,128)(2,1)S(1)}, bf16[128,8192]{1,0:T(8,128)(2,1)S(1)}, u32[]{:S(2)}, u32[]{:S(2)}) collective-permute-start(bf16[128,8192]{1,0:T(8,128)(2,1)S(1)} %get-tuple-element.48), channel_id=1, source_target_pairs={{0,2},{1,3},{2,0},{3,1},{4,6},{5,7},{6,4},{7,5},{8,10},{9,11},{10,... | collective-permute-start | bytes 6291464 | tf_op jit(solution)/shard_map/ppermute | solution.py:24
  13.4 3.3 %copy-start.1 = (bf16[8192,512]{1,0:T(8,128)(2,1)}, bf16[8192,512]{1,0:T(8,128)(2,1)S(1)}, u32[]{:S(2)}) copy-start(bf16[8192,512]{1,0:T(8,128)(2,1)S(1)} %collective-permute-done.1.refs_1_) | copy-start | bytes 25165828
  23.5 96.9 %collective-permute-start.13 = (bf16[128,8192]{1,0:T(8,128)(2,1)}, bf16[128,8192]{1,0:T(8,128)(2,1)}, u32[]{:S(2)}, u32[]{:S(2)}) collective-permute-start(bf16[128,8192]{1,0:T(8,128)(2,1)} %get-tuple-element.38), channel_id=1, source_target_pairs={{0,2},{1,3},{2,0},{3,1},{4,6},{5,7},{6,4},{7,5},{8,10},{9,11},{10,... | collective-permute-start | bytes 6291464 | tf_op jit(solution)/shard_map/ppermute | solution.py:24
  26.4 27.2 %collective-permute-start.3 = (bf16[256,1024]{1,0:T(8,128)(2,1)S(1)}, bf16[256,1024]{1,0:T(8,128)(2,1)S(1)}, u32[]{:S(2)}, u32[]{:S(2)}) collective-permute-start(bf16[256,1024]{1,0:T(8,128)(2,1)S(1)} %shard_map.55.refs_0_), channel_id=1, source_target_pairs={{0,24},{1,25},{2,26},{3,27},{4,28},{5,29},{6,30},{7,31},{8,0},{9,1... | collective-permute-start | bytes 1572872 | tf_op jit(solution)/shard_map/ppermute | solution.py:33
  30.0 23.6 %collective-permute-start.2 = (bf16[256,1024]{1,0:T(8,128)(2,1)S(1)}, bf16[256,1024]{1,0:T(8,128)(2,1)S(1)}, u32[]{:S(2)}, u32[]{:S(2)}) collective-permute-start(bf16[256,1024]{1,0:T(8,128)(2,1)S(1)} %shard_map.55.refs_0_), channel_id=1, source_target_pairs={{0,8},{1,9},{2,10},{3,11},{4,12},{5,13},{6,14},{7,15},{8,16},{9,17... | collective-permute-start | bytes 1572872 | tf_op jit(solution)/shard_map/ppermute | solution.py:33
  30.1 25.7 %collective-permute-start.5 = (bf16[256,1024]{1,0:T(8,128)(2,1)S(1)}, bf16[256,1024]{1,0:T(8,128)(2,1)S(1)}, u32[]{:S(2)}, u32[]{:S(2)}) collective-permute-start(bf16[256,1024]{1,0:T(8,128)(2,1)S(1)} %shard_map.55.refs_0_), channel_id=1, source_target_pairs={{0,4},{4,0},{8,12},{12,8},{16,20},{20,16},{24,28},{28,24},{1,5},{5... | collective-permute-start | bytes 1572872 | tf_op jit(solution)/shard_map/ppermute | solution.py:24
  53.7 38.9 %copy-start.3 = (s32[8,16]{1,0:T(8,128)S(1)}, s32[8,16]{1,0:T(8,128)}, u32[]{:S(2)}) copy-start(s32[8,16]{1,0:T(8,128)} %param.9) | copy-start | bytes 1540
  53.7 39.0 %copy-start.2 = (s32[8,16,8]{1,2,0:T(8,128)S(1)}, s32[8,16,8]{1,2,0:T(8,128)}, u32[]{:S(2)}) copy-start(s32[8,16,8]{1,2,0:T(8,128)} %param.8) | copy-start | bytes 12292
  53.7 36.8 %collective-permute-start.12 = (bf16[512,1024]{1,0:T(8,128)(2,1)S(1)}, bf16[512,1024]{1,0:T(8,128)(2,1)S(1)}, u32[]{:S(2)}, u32[]{:S(2)}) collective-permute-start(bf16[512,1024]{1,0:T(8,128)(2,1)S(1)} %pad_maximum_fusion.1), channel_id=1, source_target_pairs={{0,4},{4,0},{8,12},{12,8},{16,20},{20,16},{24,28},{28,24},{1,5},{5... | collective-permute-start | bytes 3145736 | tf_op jit(solution)/shard_map/ppermute | solution.py:24
  55.7 30.8 %collective-permute-start.6 = (bf16[256,1024]{1,0:T(8,128)(2,1)S(1)}, bf16[256,1024]{1,0:T(8,128)(2,1)}, u32[]{:S(2)}, u32[]{:S(2)}) collective-permute-start(bf16[256,1024]{1,0:T(8,128)(2,1)S(1)} %shard_map.55.refs_0_), channel_id=1, source_target_pairs={{0,16},{1,17},{2,18},{3,19},{4,20},{5,21},{6,22},{7,23},{8,24},{9,... | collective-permute-start | bytes 1572872 | tf_op jit(solution)/shard_map/ppermute | solution.py:33
  64.6 12.7 %collective-permute-start.4 = (bf16[128,1024]{1,0:T(8,128)(2,1)S(1)}, bf16[128,1024]{1,0:T(8,128)(2,1)S(1)}, u32[]{:S(2)}, u32[]{:S(2)}) collective-permute-start(bf16[128,1024]{1,0:T(8,128)(2,1)S(1)} %shard_map.56), channel_id=1, source_target_pairs={{0,10},{1,11},{2,8},{3,9},{4,14},{5,15},{6,12},{7,13},{8,18},{9,19... | collective-permute-start | bytes 786440 | tf_op jit(solution)/shard_map/ppermute | solution.py:33
  86.5 22.9 %collective-permute-start.7 = (bf16[256,1024]{1,0:T(8,128)(2,1)}, bf16[256,1024]{1,0:T(8,128)(2,1)}, u32[]{:S(2)}, u32[]{:S(2)}) collective-permute-start(bf16[256,1024]{1,0:T(8,128)(2,1)} %collective-permute-done.6.refs_3_), channel_id=1, source_target_pairs={{0,4},{4,0},{8,12},{12,8},{16,20},{20,16},{24,28},{28,24},{1,5},{5... | collective-permute-start | bytes 1572872 | tf_op jit(solution)/shard_map/ppermute | solution.py:24
  87.0 16.1 %collective-permute-start.10 = (bf16[128,1024]{1,0:T(8,128)(2,1)S(1)}, bf16[128,1024]{1,0:T(8,128)(2,1)}, u32[]{:S(2)}, u32[]{:S(2)}) collective-permute-start(bf16[128,1024]{1,0:T(8,128)(2,1)S(1)} %collective-permute-done.4.refs_0_), channel_id=1, source_target_pairs={{0,16},{1,17},{2,18},{3,19},{4,20},{5,21},{6,22},{7,23},{8,24},{9,... | collective-permute-start | bytes 786440 | tf_op jit(solution)/shard_map/ppermute | solution.py:33
  90.5 18.8 %collective-permute-start.9 = (bf16[128,1024]{1,0:T(8,128)(2,1)S(1)}, bf16[128,1024]{1,0:T(8,128)(2,1)}, u32[]{:S(2)}, u32[]{:S(2)}) collective-permute-start(bf16[128,1024]{1,0:T(8,128)(2,1)S(1)} %collective-permute-done.4.refs_0_), channel_id=1, source_target_pairs={{0,24},{1,25},{2,26},{3,27},{4,28},{5,29},{6,30},{7,31},{8,0},{9,1... | collective-permute-start | bytes 786440 | tf_op jit(solution)/shard_map/ppermute | solution.py:33
  90.5 18.8 %collective-permute-start.8 = (bf16[128,1024]{1,0:T(8,128)(2,1)S(1)}, bf16[128,1024]{1,0:T(8,128)(2,1)}, u32[]{:S(2)}, u32[]{:S(2)}) collective-permute-start(bf16[128,1024]{1,0:T(8,128)(2,1)S(1)} %collective-permute-done.4.refs_0_), channel_id=1, source_target_pairs={{0,8},{1,9},{2,10},{3,11},{4,12},{5,13},{6,14},{7,15},{8,16},{9,17... | collective-permute-start | bytes 786440 | tf_op jit(solution)/shard_map/ppermute | solution.py:33
  129.0 14.1 %collective-permute-start.14 = (bf16[128,1024]{1,0:T(8,128)(2,1)}, bf16[128,1024]{1,0:T(8,128)(2,1)}, u32[]{:S(2)}, u32[]{:S(2)}) collective-permute-start(bf16[128,1024]{1,0:T(8,128)(2,1)} %shard_map.59), channel_id=1, source_target_pairs={{0,2},{1,3},{2,0},{3,1},{4,6},{5,7},{6,4},{7,5},{8,10},{9,11},{10,... | collective-permute-start | bytes 786440 | tf_op jit(solution)/shard_map/ppermute | solution.py:24
  132.2 37.1 %collective-permute-start.11 = (bf16[512,1024]{1,0:T(8,128)(2,1)}, bf16[512,1024]{1,0:T(8,128)(2,1)}, u32[]{:S(2)}, u32[]{:S(2)}) collective-permute-start(bf16[512,1024]{1,0:T(8,128)(2,1)} %pad_maximum_fusion), channel_id=1, source_target_pairs={{0,4},{4,0},{8,12},{12,8},{16,20},{20,16},{24,28},{28,24},{1,5},{5... | collective-permute-start | bytes 3145736 | tf_op jit(solution)/shard_map/ppermute | solution.py:24
  144.0 12.1 %collective-permute-start.15 = (bf16[48,1024]{1,0:T(8,128)(2,1)S(1)}, bf16[48,1024]{1,0:T(8,128)(2,1)S(1)}, u32[]{:S(2)}, u32[]{:S(2)}) collective-permute-start(bf16[48,1024]{1,0:T(8,128)(2,1)S(1)} %slice.26), channel_id=1, source_target_pairs={{0,4},{4,0},{8,12},{12,8},{16,20},{20,16},{24,28},{28,24},{1,5},{5... | collective-permute-start | bytes 294920 | tf_op jit(solution)/shard_map/ppermute | solution.py:24
  145.8 14.6 %collective-permute-start.18 = (bf16[80,1024]{1,0:T(8,128)(2,1)S(1)}, bf16[80,1024]{1,0:T(8,128)(2,1)S(1)}, u32[]{:S(2)}, u32[]{:S(2)}) collective-permute-start(bf16[80,1024]{1,0:T(8,128)(2,1)S(1)} %slice.25.refs_5_), channel_id=1, source_target_pairs={{0,16},{1,17},{2,18},{3,19},{4,20},{5,21},{6,22},{7,23},{8,24},{9,... | collective-permute-start | bytes 491528 | tf_op jit(solution)/shard_map/ppermute | solution.py:33
  151.3 9.1 %collective-permute-start.17 = (bf16[80,1024]{1,0:T(8,128)(2,1)S(1)}, bf16[80,1024]{1,0:T(8,128)(2,1)S(1)}, u32[]{:S(2)}, u32[]{:S(2)}) collective-permute-start(bf16[80,1024]{1,0:T(8,128)(2,1)S(1)} %slice.25.refs_5_), channel_id=1, source_target_pairs={{0,24},{1,25},{2,26},{3,27},{4,28},{5,29},{6,30},{7,31},{8,0},{9,1... | collective-permute-start | bytes 491528 | tf_op jit(solution)/shard_map/ppermute | solution.py:33
  153.6 9.6 %collective-permute-start.16 = (bf16[80,1024]{1,0:T(8,128)(2,1)S(1)}, bf16[80,1024]{1,0:T(8,128)(2,1)S(1)}, u32[]{:S(2)}, u32[]{:S(2)}) collective-permute-start(bf16[80,1024]{1,0:T(8,128)(2,1)S(1)} %slice.25.refs_5_), channel_id=1, source_target_pairs={{0,8},{1,9},{2,10},{3,11},{4,12},{5,13},{6,14},{7,15},{8,16},{9,17... | collective-permute-start | bytes 491528 | tf_op jit(solution)/shard_map/ppermute | solution.py:33
  163.2 17.3 %collective-permute-start.19 = (bf16[320,1024]{1,0:T(8,128)(2,1)S(1)}, bf16[320,1024]{1,0:T(8,128)(2,1)S(1)}, u32[]{:S(2)}, u32[]{:S(2)}) collective-permute-start(bf16[320,1024]{1,0:T(8,128)(2,1)S(1)} %pad_maximum_fusion.2), channel_id=1, source_target_pairs={{0,4},{4,0},{8,12},{12,8},{16,20},{20,16},{24,28},{28,24},{1,5},{5... | collective-permute-start | bytes 1966088 | tf_op jit(solution)/shard_map/ppermute | solution.py:24
  164.6 12.9 %collective-permute-start.22 = (bf16[96,1024]{1,0:T(8,128)(2,1)S(1)}, bf16[96,1024]{1,0:T(8,128)(2,1)S(1)}, u32[]{:S(2)}, u32[]{:S(2)}) collective-permute-start(bf16[96,1024]{1,0:T(8,128)(2,1)S(1)} %pad_maximum_fusion.3.refs_10_), channel_id=1, source_target_pairs={{0,16},{1,17},{2,18},{3,19},{4,20},{5,21},{6,22},{7,23},{8,24},{9,... | collective-permute-start | bytes 589832 | tf_op jit(solution)/shard_map/ppermute | solution.py:33
  167.2 13.4 %collective-permute-start.21 = (bf16[96,1024]{1,0:T(8,128)(2,1)S(1)}, bf16[96,1024]{1,0:T(8,128)(2,1)S(1)}, u32[]{:S(2)}, u32[]{:S(2)}) collective-permute-start(bf16[96,1024]{1,0:T(8,128)(2,1)S(1)} %pad_maximum_fusion.3.refs_10_), channel_id=1, source_target_pairs={{0,24},{1,25},{2,26},{3,27},{4,28},{5,29},{6,30},{7,31},{8,0},{9,1... | collective-permute-start | bytes 589832 | tf_op jit(solution)/shard_map/ppermute | solution.py:33
  168.1 12.4 %collective-permute-start.20 = (bf16[96,1024]{1,0:T(8,128)(2,1)S(1)}, bf16[96,1024]{1,0:T(8,128)(2,1)S(1)}, u32[]{:S(2)}, u32[]{:S(2)}) collective-permute-start(bf16[96,1024]{1,0:T(8,128)(2,1)S(1)} %pad_maximum_fusion.3.refs_10_), channel_id=1, source_target_pairs={{0,8},{1,9},{2,10},{3,11},{4,12},{5,13},{6,14},{7,15},{8,16},{9,17... | collective-permute-start | bytes 589832 | tf_op jit(solution)/shard_map/ppermute | solution.py:33
